TPU v7x, 512 devices: a whole 4x4x16 slice. The times are simulated.
512 devices in a mesh: ep: 128 (over z, y, core), dp: 4 (over x).
Axes of the slice: x: 4, y: 4, z: 16, core: 2. Of those that a mesh axis runs over, the one named last changes fastest.
Arguments:
- out_grads: bfloat16 [65536, 2048], P(('ep', 'dp')), may hold values from -40 to 40
- hidden_acts: bfloat16 [65536, 512], P(('ep', 'dp')), may hold values from -20 to 20
- routing: int32 [65536, 1], P(('ep', 'dp')), may hold values from 0 to 95, as said below
- replica_pick: int32 [65536], P(('ep', 'dp')), may hold values from 0 to 3
- master_weights: float32 [128, 2048, 512], P('ep', 'dp'), may hold values from -0.25 to 0.25
- current_slots: int32 [128], replicated, may hold values from 0 to 95, as said below
- next_slots: int32 [128], replicated, may hold values from 0 to 95, as said below
Outputs:
- input_grads: float32 [65536, 512], P(('ep', 'dp'))
- moved_weights: float32 [128, 2048, 512], P('ep', 'dp')
- moved_updates: float32 [128, 2048, 512], P('ep', 'dp')
Inputs may be any that keep to these rules, and one draw needn't show every extreme that they name: `routing`: the rows of one device name each expert at most 2 times; the experts held by two slots now are named exactly 2 times by the rows of every device. `current_slots`: every expert below 96 is held by one or two slots. `next_slots`: every expert below 96 is held by at least one slot.
All inputs are finite; a program needn't handle non-finite values.
Results may differ from a plain program's by a relative error of at most 0.0029.
Values may be sent and summed in bfloat16 or wider, within the bound.
A program may use at most 64 MiB of HBM per device.

v0:
```python
import jax
import jax.numpy as jnp
from jax import lax
from jax.sharding import PartitionSpec as P

D = 2048
NS_STEPS = 2
POLY_FIRST = 3.4445
POLY_SECOND = -4.775
POLY_THIRD = 2.0315
LEARNING_RATE = 0.02
UPDATE_SCALE = 0.2
EPSILON = 1e-07
PRECISE = lax.Precision.HIGHEST


def slot_ranks(placement):
    number = placement.shape[0]
    matching = placement[:, None] == placement[None, :]
    earlier = (
        jnp.arange(number, dtype=jnp.int32)[None, :] < jnp.arange(number, dtype=jnp.int32)[:, None]
    )
    return jnp.sum(matching & earlier, axis=1)


def choose_slots(placement, rankings, experts_named, wanted_index):
    holders = placement[None, :] == experts_named[:, None]
    totals = jnp.sum(holders, axis=1)
    wanted = jnp.remainder(wanted_index, totals)
    chosen = holders & (rankings[None, :] == wanted[:, None])
    ordinal = jnp.arange(placement.shape[0], dtype=jnp.int32)[None, :]
    return jnp.sum(jnp.where(chosen, ordinal, 0), axis=1)


def gram_of(matrix):
    return lax.dot_general(matrix, matrix, (((0,), (0,)), ((), ())), precision=PRECISE)


def orthogonalize(grad):
    squares = lax.psum(jnp.sum(grad * grad), "dp")
    normed = grad / (jnp.sqrt(squares) + EPSILON)
    gram_now = lax.psum(gram_of(normed), "dp")
    for iteration in range(NS_STEPS):
        if iteration > 0:
            gram_now = lax.psum(gram_of(normed), "dp")
        polynomial = POLY_SECOND * gram_now + POLY_THIRD * jnp.dot(
            gram_now, gram_now, precision=PRECISE
        )
        normed = POLY_FIRST * normed + jnp.dot(normed, polynomial, precision=PRECISE)
    return UPDATE_SCALE * D**0.5 * normed


def per_device(
    out_grads, hidden_acts, routing, replica_pick, master_weights, current_slots, next_slots
):
    tok_rows = out_grads.shape[0]
    model_width = out_grads.shape[1]
    expert_width = hidden_acts.shape[1]
    ep_size = lax.axis_size("ep")
    capacity = 2 * tok_rows // ep_size
    local_master = master_weights[0]
    rankings = slot_ranks(current_slots)
    slot_of_row = choose_slots(current_slots, rankings, routing[:, 0], replica_pick)
    onehot_slots = (slot_of_row[:, None] == jnp.arange(ep_size, dtype=jnp.int32)[None, :]).astype(
        jnp.int32
    )
    running = jnp.cumsum(onehot_slots, axis=0)
    position = jnp.sum(onehot_slots * (running - 1), axis=1)
    target = slot_of_row * capacity + position
    send_grads = (
        jnp.zeros((ep_size * capacity, model_width), jnp.bfloat16).at[target].set(out_grads)
    )
    send_acts = (
        jnp.zeros((ep_size * capacity, expert_width), jnp.bfloat16).at[target].set(hidden_acts)
    )
    recv_grads, recv_acts = (
        lax.all_to_all(
            send_grads.reshape(ep_size, capacity, model_width),
            "ep",
            split_axis=0,
            concat_axis=0,
            tiled=True,
        ),
        lax.all_to_all(
            send_acts.reshape(ep_size, capacity, expert_width),
            "ep",
            split_axis=0,
            concat_axis=0,
            tiled=True,
        ),
    )
    rows_grads = recv_grads.reshape(-1, model_width)
    rows_acts = recv_acts.reshape(-1, expert_width)
    weight_copy = local_master.astype(jnp.bfloat16)
    columns = rows_grads
    gathered = jnp.dot(
        columns,
        lax.all_gather(weight_copy, "dp", axis=0, tiled=True),
        preferred_element_type=jnp.float32,
    )
    returned = lax.all_to_all(
        gathered.reshape(ep_size, capacity, expert_width),
        "ep",
        split_axis=0,
        concat_axis=0,
        tiled=True,
    )
    input_grads = returned.reshape(-1, expert_width)[target]
    columns = rows_grads
    slot_grad = lax.psum_scatter(
        lax.dot_general(
            columns, rows_acts, (((0,), (0,)), ((), ())), preferred_element_type=jnp.float32
        ),
        "dp",
        scatter_dimension=0,
        tiled=True,
    )
    piece_len = local_master.shape[0] * local_master.shape[1] // ep_size
    homes_next = choose_slots(current_slots, rankings, next_slots, jnp.zeros_like(next_slots))
    matching = (current_slots[:, None] == current_slots[None, :]).astype(jnp.float32)
    spread = lax.all_to_all(
        slot_grad.reshape(ep_size, piece_len), "ep", split_axis=0, concat_axis=0, tiled=True
    )
    summed = jnp.dot(matching, spread, precision=PRECISE)
    expert_grad = lax.all_to_all(summed, "ep", split_axis=0, concat_axis=0, tiled=True).reshape(
        local_master.shape
    )
    update = orthogonalize(expert_grad)
    fresh = local_master - LEARNING_RATE * update
    pieces_weight, pieces_update = (
        lax.all_to_all(
            fresh.reshape(ep_size, piece_len), "ep", split_axis=0, concat_axis=0, tiled=True
        ),
        lax.all_to_all(
            update.reshape(ep_size, piece_len), "ep", split_axis=0, concat_axis=0, tiled=True
        ),
    )
    chosen_weight = jnp.take(pieces_weight, homes_next, axis=0)
    chosen_update = jnp.take(pieces_update, homes_next, axis=0)
    arrived_weight, arrived_update = (
        lax.all_to_all(chosen_weight, "ep", split_axis=0, concat_axis=0, tiled=True),
        lax.all_to_all(chosen_update, "ep", split_axis=0, concat_axis=0, tiled=True),
    )
    moved_weight = arrived_weight.reshape(local_master.shape)
    moved_update = arrived_update.reshape(local_master.shape)
    return (input_grads, moved_weight[None], moved_update[None])


def solution(mesh):
    placed = (
        P(("ep", "dp"), None),
        P(("ep", "dp"), None),
        P(("ep", "dp"), None),
        P(("ep", "dp")),
        P("ep", "dp", None),
        P(),
        P(),
    )
    return jax.shard_map(
        per_device,
        mesh=mesh,
        in_specs=placed,
        out_specs=(P(("ep", "dp"), None), P("ep", "dp", None), P("ep", "dp", None)),
        check_vma=False,
    )
```

profile of v0, /device:TPU:33, one launch (start us, length us, event | category | flops | bytes accessed | tf_op | source)
XLA Modules:
  0.0 765.5 jit_solution(6440641814367399283)
XLA Ops:
  14.0 19.5 %all-to-all-start = ((bf16[128,2,2048]{2,1,0:T(2,128)(2,1)}), bf16[128,2,2048]{2,1,0:T(2,128)(2,1)S(1)}, u32[]{:S(2)}, u32[]{:S(2)}) async-start(bf16[128,2,2048]{2,1,0:T(2,128)(2,1)} %reshape.99), calls=%async_computation | async-start | bytes 2097152 | tf_op jit(solution)/shard_map/all_to_all | solution.py:77
  35.8 53.3 %all-to-all-done = bf16[128,2,2048]{2,1,0:T(2,128)(2,1)S(1)} async-done(((bf16[128,2,2048]{2,1,0:T(2,128)(2,1)}), bf16[128,2,2048]{2,1,0:T(2,128)(2,1)S(1)}, u32[]{:S(2)}, u32[]{:S(2)}) %all-to-all-start) | async-done | bytes 1048608 | tf_op jit(solution)/shard_map/all_to_all | solution.py:77
  89.1 6.4 all-to-all-start.2
  96.6 21.5 %all-to-all-done.2 = bf16[128,2,512]{2,1,0:T(2,128)(2,1)S(1)} async-done(((bf16[128,2,512]{2,1,0:T(2,128)(2,1)}), bf16[128,2,512]{2,1,0:T(2,128)(2,1)S(1)}, u32[]{:S(2)}, u32[]{:S(2)}) %all-to-all-start.2) | async-done | bytes 262176 | tf_op jit(solution)/shard_map/all_to_all | solution.py:84
  120.8 45.4 %reduce-scatter.2.cloned.1.call-done = f32[512,512]{1,0:T(8,128)} async-done(((f32[2048,512]{1,0:T(8,128)}), f32[512,512]{1,0:T(8,128)}) %reduce-scatter.2.cloned.1.call-update) | async-done | bytes 1048592 | tf_op jit(solution)/shard_map/reduce_scatter | solution.py:110
  168.8 72.3 %all_to_all.81 = f32[128,1,2048]{2,1,0:T(1,128)S(1)} all-to-all(f32[128,1,2048]{2,1,0:T(1,128)S(1)} %all_to_all.69), channel_id=1, replica_groups=mesh['ep'=128,'dp'=4] {'ep'}, dimensions={0} | all-to-all | bytes 2097152 | tf_op jit(solution)/shard_map/all_to_all | solution.py:121
  243.1 61.9 %all_to_all.82 = f32[128,1,2048]{2,1,0:T(1,128)S(1)} all-to-all(f32[128,1,2048]{2,1,0:T(1,128)S(1)} %copy.20), channel_id=1, replica_groups=mesh['ep'=128,'dp'=4] {'ep'}, dimensions={0} | all-to-all | bytes 2097152 | tf_op jit(solution)/shard_map/all_to_all | solution.py:125
  307.7 7.2 psum.21
  321.7 50.9 %all-reduce.3.cloned.1.call-done = f32[512,512]{1,0:T(8,128)} async-done(((f32[512,512]{1,0:T(8,128)}), f32[512,512]{1,0:T(8,128)}) %all-reduce.3.cloned.1.call-update) | async-done | bytes 1048592 | tf_op jit(solution)/shard_map/psum | solution.py:42
  372.6 3.9 fusion.3
  381.2 62.3 %all-reduce.5.cloned.1.call-done = f32[512,512]{1,0:T(8,128)} async-done(((f32[512,512]{1,0:T(8,128)}), f32[512,512]{1,0:T(8,128)}) %all-reduce.5.cloned.1.call-update) | async-done | bytes 1048592 | tf_op jit(solution)/shard_map/psum | solution.py:45
  443.5 3.9 fusion.2
  450.8 3.6 all_to_all.71
  454.3 18.6 %all-to-all-start.7 = ((f32[128,1,2048]{2,1,0:T(1,128)}), f32[128,1,2048]{2,1,0:T(1,128)}, u32[]{:S(2)}, u32[]{:S(2)}) async-start(f32[128,1,2048]{2,1,0:T(1,128)} %all_to_all.71), calls=%async_computation.8 | async-start | bytes 2097152 | tf_op jit(solution)/shard_map/all_to_all | solution.py:134
  475.2 53.0 %all-to-all-done.7 = f32[128,1,2048]{2,1,0:T(1,128)} async-done(((f32[128,1,2048]{2,1,0:T(1,128)}), f32[128,1,2048]{2,1,0:T(1,128)}, u32[]{:S(2)}, u32[]{:S(2)}) %all-to-all-start.7) | async-done | bytes 1048608 | tf_op jit(solution)/shard_map/all_to_all | solution.py:134
  528.2 6.4 all-to-all-start.5
  535.6 41.3 %all-gather.2.cloned.1.call-done = bf16[2048,512]{1,0:T(8,128)(2,1)} async-done(((bf16[512,512]{1,0:T(8,128)(2,1)}), bf16[2048,512]{1,0:T(8,128)(2,1)}) %all-gather.2.cloned.1.call-update) | async-done | bytes 2097168 | tf_op jit(solution)/shard_map/all_gather | solution.py:98
  580.4 9.9 %all-to-all-done.5 = f32[128,1,2048]{2,1,0:T(1,128)S(1)} async-done(((f32[128,1,2048]{2,1,0:T(1,128)}), f32[128,1,2048]{2,1,0:T(1,128)S(1)}, u32[]{:S(2)}, u32[]{:S(2)}) %all-to-all-start.5) | async-done | bytes 1048608 | tf_op jit(solution)/shard_map/all_to_all | solution.py:131
  590.3 7.3 all-to-all-start.1
  603.8 27.0 %all-to-all-done.1 = f32[128,2,512]{2,1,0:T(2,128)} async-done(((f32[128,2,512]{2,1,0:T(2,128)}), f32[128,2,512]{2,1,0:T(2,128)}, u32[]{:S(2)}, u32[]{:S(2)}) %all-to-all-start.1) | async-done | bytes 524320 | tf_op jit(solution)/shard_map/all_to_all | solution.py:101
  630.9 6.6 all-to-all-start.6
  639.6 53.4 %all-to-all-done.6 = f32[128,1,2048]{2,1,0:T(1,128)S(1)} async-done(((f32[128,1,2048]{2,1,0:T(1,128)}), f32[128,1,2048]{2,1,0:T(1,128)S(1)}, u32[]{:S(2)}, u32[]{:S(2)}) %all-to-all-start.6) | async-done | bytes 1048608 | tf_op jit(solution)/shard_map/all_to_all | solution.py:141
  693.0 6.4 all-to-all-start.8
  706.1 49.0 %all-to-all-done.8 = f32[128,1,2048]{2,1,0:T(1,128)S(1)} async-done(((f32[128,1,2048]{2,1,0:T(1,128)}), f32[128,1,2048]{2,1,0:T(1,128)S(1)}, u32[]{:S(2)}, u32[]{:S(2)}) %all-to-all-start.8) | async-done | bytes 1048608 | tf_op jit(solution)/shard_map/all_to_all | solution.py:142
  (58 shorter events, 59.4 us)
Async XLA Ops:
  14.0 75.1 %all-to-all-start = ((bf16[128,2,2048]{2,1,0:T(2,128)(2,1)}), bf16[128,2,2048]{2,1,0:T(2,128)(2,1)S(1)}, u32[]{:S(2)}, u32[]{:S(2)}) async-start(bf16[128,2,2048]{2,1,0:T(2,128)(2,1)} %reshape.99), calls=%async_computation | async-start | bytes 2097152 | tf_op jit(solution)/shard_map/all_to_all | solution.py:77
  89.1 29.0 %all-to-all-start.2 = ((bf16[128,2,512]{2,1,0:T(2,128)(2,1)}), bf16[128,2,512]{2,1,0:T(2,128)(2,1)S(1)}, u32[]{:S(2)}, u32[]{:S(2)}) async-start(bf16[128,2,512]{2,1,0:T(2,128)(2,1)} %reshape.101), calls=%async_computation.2 | async-start | bytes 524288 | tf_op jit(solution)/shard_map/all_to_all | solution.py:84
  95.6 70.7 %reduce-scatter.2.cloned.1.call-start = ((), (), s32[]{:S(2)}) async-start(), calls=%async_computation.11 | async-start | bytes 5242880 | tf_op jit(solution)/shard_map/reduce_scatter | solution.py:110
  120.8 120.3 %copy-start.2 = (s32[128]{0:T(128)S(1)}, s32[128]{0:T(128)}, u32[]{:S(2)}) copy-start(s32[128]{0:T(128)} %param.14) | copy-start | bytes 1540
  120.8 251.8 %all-reduce.3.cloned.1.call-start = ((), (), s32[]{:S(2)}) async-start(), calls=%async_computation.12 | async-start | bytes 2097152 | tf_op jit(solution)/shard_map/psum | solution.py:42
  321.4 122.1 %all-reduce.5.cloned.1.call-start = ((), (), s32[]{:S(2)}) async-start(), calls=%async_computation.13 | async-start | bytes 2097152 | tf_op jit(solution)/shard_map/psum | solution.py:45
  381.2 66.3 %copy-start = (f32[1,512,512]{2,1,0:T(8,128)S(1)}, f32[1,512,512]{2,1,0:T(8,128)}, u32[]{:S(2)}) copy-start(f32[1,512,512]{2,1,0:T(8,128)} %param.13) | copy-start | bytes 3145732
  450.8 22.2 %copy-start.1 = (f32[512,512]{1,0:T(8,128)S(1)}, f32[512,512]{1,0:T(8,128)}, u32[]{:S(2)}) copy-start(f32[512,512]{1,0:T(8,128)} %get-tuple-element.10) | copy-start | bytes 3145732
  454.3 73.9 %all-to-all-start.7 = ((f32[128,1,2048]{2,1,0:T(1,128)}), f32[128,1,2048]{2,1,0:T(1,128)}, u32[]{:S(2)}, u32[]{:S(2)}) async-start(f32[128,1,2048]{2,1,0:T(1,128)} %all_to_all.71), calls=%async_computation.8 | async-start | bytes 2097152 | tf_op jit(solution)/shard_map/all_to_all | solution.py:134
  528.2 62.1 %all-to-all-start.5 = ((f32[128,1,2048]{2,1,0:T(1,128)}), f32[128,1,2048]{2,1,0:T(1,128)S(1)}, u32[]{:S(2)}, u32[]{:S(2)}) async-start(f32[128,1,2048]{2,1,0:T(1,128)} %all_to_all.70), calls=%async_computation.6 | async-start | bytes 2097152 | tf_op jit(solution)/shard_map/all_to_all | solution.py:131
  534.7 42.2 %all-gather.2.cloned.1.call-start = ((), (), s32[]{:S(2)}) async-start(), calls=%async_computation.10 | async-start | bytes 2621440 | tf_op jit(solution)/shard_map/all_gather | solution.py:98
  590.3 40.6 %all-to-all-start.1 = ((f32[128,2,512]{2,1,0:T(2,128)}), f32[128,2,512]{2,1,0:T(2,128)}, u32[]{:S(2)}, u32[]{:S(2)}) async-start(f32[128,2,512]{2,1,0:T(2,128)} %copy.16), calls=%async_computation.1 | async-start | bytes 1048576 | tf_op jit(solution)/shard_map/all_to_all | solution.py:101
  630.9 62.1 %all-to-all-start.6 = ((f32[128,1,2048]{2,1,0:T(1,128)}), f32[128,1,2048]{2,1,0:T(1,128)S(1)}, u32[]{:S(2)}, u32[]{:S(2)}) async-start(f32[128,1,2048]{2,1,0:T(1,128)} %copy.22), calls=%async_computation.7 | async-start | bytes 2097152 | tf_op jit(solution)/shard_map/all_to_all | solution.py:141
  693.0 62.1 %all-to-all-start.8 = ((f32[128,1,2048]{2,1,0:T(1,128)}), f32[128,1,2048]{2,1,0:T(1,128)S(1)}, u32[]{:S(2)}, u32[]{:S(2)}) async-start(f32[128,1,2048]{2,1,0:T(1,128)} %copy.24), calls=%async_computation.9 | async-start | bytes 2097152 | tf_op jit(solution)/shard_map/all_to_all | solution.py:142
Sparse Core Ops, SparseCore 0:
  120.9 45.3 reduce-scatter.1
  321.5 51.0 all-reduce.2
  381.3 62.1 all-reduce.4
  538.1 38.7 all-gather.1
where the time goes:
time: 774 us; the launch traced here: 766 us
  waiting for transfers between devices  467 us (60%)
  blocking collectives  141 us (18%)
  starting transfers between devices  71.7 us (9%)
  local copies, waits for them, and re-layouts  31.3 us (4%)
  matrix products  24.6 us (3%)
  between operations  14.9 us (2%)
  other arithmetic  14.6 us (2%)
    psum x2, waiting for transfers between devices, orthogonalize(): gram_now = lax.psum(gram_of(normed), 'dp')  113 us
    all_to_all x1, blocking collectives, per_device(): lax.all_to_all(slot_grad.reshape(ep_size, piece_len), 'ep', split_axis=0,...  72.3 us
    all_to_all x1, blocking collectives, per_device(): lax.all_to_all(summed, 'ep', split_axis=0, concat_axis=0, tiled=True)  61.9 us
    all_to_all x1, waiting for transfers between devices, per_device(): lax.all_to_all(chosen_weight, 'ep', split_axis=0, concat_axis=0, tiled=True)  53.4 us
    all_to_all x1, waiting for transfers between devices, per_device(): lax.all_to_all(send_grads.reshape(ep_size, capacity, model_width), 'ep',...  53.3 us
    all_to_all x1, waiting for transfers between devices, per_device(): lax.all_to_all(update.reshape(ep_size, piece_len), 'ep', split_axis=0, co...  53 us
    all_to_all x1, waiting for transfers between devices, per_device(): lax.all_to_all(chosen_update, 'ep', split_axis=0, concat_axis=0, tiled=True)  49 us
    reduce_scatter x1, waiting for transfers between devices, per_device(): lax.psum_scatter(lax.dot_general(columns, rows_acts, (((0,), (0,)), ((),...  45.4 us
  transfers between devices with their start and end apart: 11, of which 11 were waited for; matrix products, arithmetic and copies ran while one was open for 3% of the time, Pallas kernels for 0%

commit v1 on v0

--- a/solution.py
+++ b/solution.py
@@ -12,6 +12,18 @@
 UPDATE_SCALE = 0.2
 EPSILON = 1e-07
 PRECISE = lax.Precision.HIGHEST
+
+
+def ring_gather(shard, axis, dim):
+    ways, here, hop = (lax.axis_size(axis), lax.axis_index(axis), shard.shape[dim])
+    shape = [n * ways if d == dim else n for d, n in enumerate(shard.shape)]
+    full = lax.dynamic_update_slice_in_dim(
+        jnp.zeros(shape, shard.dtype), shard, here * hop, axis=dim
+    )
+    for far in range(1, ways):
+        shard = lax.ppermute(shard, axis, [(d, (d + 1) % ways) for d in range(ways)])
+        full = lax.dynamic_update_slice_in_dim(full, shard, (here - far) % ways * hop, axis=dim)
+    return full
 
 
 def slot_ranks(placement):
@@ -94,9 +106,7 @@
     weight_copy = local_master.astype(jnp.bfloat16)
     columns = rows_grads
     gathered = jnp.dot(
-        columns,
-        lax.all_gather(weight_copy, "dp", axis=0, tiled=True),
-        preferred_element_type=jnp.float32,
+        columns, ring_gather(weight_copy, "dp", 0), preferred_element_type=jnp.float32
     )
     returned = lax.all_to_all(
         gathered.reshape(ep_size, capacity, expert_width),

time: 774 us -> 783 us (1.012)
  starting transfers between devices: 71.7 us -> 86.1 us
  waiting for transfers between devices: 467 us -> 458 us
    all_gather x1 -> x0, waiting for transfers between devices: 41.3 us -> none  [per_device(): lax.all_gather(weight_copy, 'dp', axis=0, tiled=True)]
    ppermute x0 -> x3, waiting for transfers between devices: none -> 38.3 us  [ring_gather(): lax.ppermute(shard, axis, [(d, (d + 1) % ways) for d in range(ways)])]
    all_to_all x1, starting transfers between devices: 7.35 us -> 15.9 us  [per_device(): lax.all_to_all(gathered.reshape(ep_size, capacity, expert_width), 'ep', s...]
  transfers between devices with their start and end apart: 11 -> 13, of which waited for: 11 -> 13; matrix products, arithmetic and copies ran while one was open for 3% -> 3% of each run, Pallas kernels for 0% -> 0%
where the time goes in v1:
time: 783 us; the launch traced here: 774 us
  waiting for transfers between devices  458 us (58%)
  blocking collectives  141 us (18%)
  starting transfers between devices  86.1 us (11%)
  local copies, waits for them, and re-layouts  35.5 us (5%)
  matrix products  23 us (3%)
  other arithmetic  15 us (2%)
  between operations  15 us (2%)
    psum x2, waiting for transfers between devices, orthogonalize(): gram_now = lax.psum(gram_of(normed), 'dp')  113 us
    all_to_all x1, blocking collectives, per_device(): lax.all_to_all(slot_grad.reshape(ep_size, piece_len), 'ep', split_axis=0,...  72.3 us
    all_to_all x1, blocking collectives, per_device(): lax.all_to_all(summed, 'ep', split_axis=0, concat_axis=0, tiled=True)  61.9 us
    all_to_all x1, waiting for transfers between devices, per_device(): lax.all_to_all(chosen_weight, 'ep', split_axis=0, concat_axis=0, tiled=True)  53.5 us
    all_to_all x1, waiting for transfers between devices, per_device(): lax.all_to_all(update.reshape(ep_size, piece_len), 'ep', split_axis=0, co...  53.4 us
    all_to_all x1, waiting for transfers between devices, per_device(): lax.all_to_all(send_grads.reshape(ep_size, capacity, model_width), 'ep',...  53.3 us
    all_to_all x1, waiting for transfers between devices, per_device(): lax.all_to_all(chosen_update, 'ep', split_axis=0, concat_axis=0, tiled=True)  49 us
    reduce_scatter x1, waiting for transfers between devices, per_device(): lax.psum_scatter(lax.dot_general(columns, rows_acts, (((0,), (0,)), ((),...  45.4 us
  transfers between devices with their start and end apart: 13, of which 13 were waited for; matrix products, arithmetic and copies ran while one was open for 3% of the time, Pallas kernels for 0%

profile of v1, /device:TPU:33, one launch (start us, length us, event | category | flops | bytes accessed | tf_op | source)
XLA Modules:
  0.0 773.9 jit_solution(11797269228071320231)
XLA Ops:
  14.0 19.5 %all-to-all-start = ((bf16[128,2,2048]{2,1,0:T(2,128)(2,1)}), bf16[128,2,2048]{2,1,0:T(2,128)(2,1)S(1)}, u32[]{:S(2)}, u32[]{:S(2)}) async-start(bf16[128,2,2048]{2,1,0:T(2,128)(2,1)} %reshape.99), calls=%async_computation | async-start | bytes 2097152 | tf_op jit(solution)/shard_map/all_to_all | solution.py:89
  35.8 53.3 %all-to-all-done = bf16[128,2,2048]{2,1,0:T(2,128)(2,1)S(1)} async-done(((bf16[128,2,2048]{2,1,0:T(2,128)(2,1)}), bf16[128,2,2048]{2,1,0:T(2,128)(2,1)S(1)}, u32[]{:S(2)}, u32[]{:S(2)}) %all-to-all-start) | async-done | bytes 1048608 | tf_op jit(solution)/shard_map/all_to_all | solution.py:89
  89.1 6.4 all-to-all-start.2
  96.6 21.5 %all-to-all-done.2 = bf16[128,2,512]{2,1,0:T(2,128)(2,1)S(1)} async-done(((bf16[128,2,512]{2,1,0:T(2,128)(2,1)}), bf16[128,2,512]{2,1,0:T(2,128)(2,1)S(1)}, u32[]{:S(2)}, u32[]{:S(2)}) %all-to-all-start.2) | async-done | bytes 262176 | tf_op jit(solution)/shard_map/all_to_all | solution.py:96
  120.8 45.4 %reduce-scatter.2.cloned.1.call-done = f32[512,512]{1,0:T(8,128)} async-done(((f32[2048,512]{1,0:T(8,128)}), f32[512,512]{1,0:T(8,128)}) %reduce-scatter.2.cloned.1.call-update) | async-done | bytes 1048592 | tf_op jit(solution)/shard_map/reduce_scatter | solution.py:120
  168.8 72.3 %all_to_all.81 = f32[128,1,2048]{2,1,0:T(1,128)S(1)} all-to-all(f32[128,1,2048]{2,1,0:T(1,128)S(1)} %all_to_all.69), channel_id=1, replica_groups=mesh['ep'=128,'dp'=4] {'ep'}, dimensions={0} | all-to-all | bytes 2097152 | tf_op jit(solution)/shard_map/all_to_all | solution.py:131
  243.1 61.9 %all_to_all.82 = f32[128,1,2048]{2,1,0:T(1,128)S(1)} all-to-all(f32[128,1,2048]{2,1,0:T(1,128)S(1)} %copy.20), channel_id=1, replica_groups=mesh['ep'=128,'dp'=4] {'ep'}, dimensions={0} | all-to-all | bytes 2097152 | tf_op jit(solution)/shard_map/all_to_all | solution.py:135
  307.7 7.2 psum.21
  321.7 50.9 %all-reduce.3.cloned.1.call-done = f32[512,512]{1,0:T(8,128)} async-done(((f32[512,512]{1,0:T(8,128)}), f32[512,512]{1,0:T(8,128)}) %all-reduce.3.cloned.1.call-update) | async-done | bytes 1048592 | tf_op jit(solution)/shard_map/psum | solution.py:54
  372.6 3.9 fusion.3
  381.2 62.3 %all-reduce.5.cloned.1.call-done = f32[512,512]{1,0:T(8,128)} async-done(((f32[512,512]{1,0:T(8,128)}), f32[512,512]{1,0:T(8,128)}) %all-reduce.5.cloned.1.call-update) | async-done | bytes 1048592 | tf_op jit(solution)/shard_map/psum | solution.py:57
  443.5 3.9 fusion.2
  454.3 18.1 %all-to-all-start.7 = ((f32[128,1,2048]{2,1,0:T(1,128)}), f32[128,1,2048]{2,1,0:T(1,128)S(1)}, u32[]{:S(2)}, u32[]{:S(2)}) async-start(f32[128,1,2048]{2,1,0:T(1,128)} %all_to_all.71), calls=%async_computation.8 | async-start | bytes 2097152 | tf_op jit(solution)/shard_map/all_to_all | solution.py:144
  474.7 53.4 %all-to-all-done.7 = f32[128,1,2048]{2,1,0:T(1,128)S(1)} async-done(((f32[128,1,2048]{2,1,0:T(1,128)}), f32[128,1,2048]{2,1,0:T(1,128)S(1)}, u32[]{:S(2)}, u32[]{:S(2)}) %all-to-all-start.7) | async-done | bytes 1048608 | tf_op jit(solution)/shard_map/all_to_all | solution.py:144
  528.1 6.9 all-to-all-start.5
  538.8 14.0 %collective-permute-done = bf16[512,512]{1,0:T(8,128)(2,1)S(1)} collective-permute-done((bf16[512,512]{1,0:T(8,128)(2,1)S(1)}, bf16[512,512]{1,0:T(8,128)(2,1)S(1)}, u32[]{:S(2)}, u32[]{:S(2)}) %collective-permute-start) | collective-permute-done | bytes 524320 | tf_op jit(solution)/shard_map/ppermute | solution.py:24
  555.6 13.6 %collective-permute-done.1 = bf16[512,512]{1,0:T(8,128)(2,1)} collective-permute-done((bf16[512,512]{1,0:T(8,128)(2,1)S(1)}, bf16[512,512]{1,0:T(8,128)(2,1)}, u32[]{:S(2)}, u32[]{:S(2)}) %collective-permute-start.1) | collective-permute-done | bytes 524320 | tf_op jit(solution)/shard_map/ppermute | solution.py:24
  573.3 10.7 %collective-permute-done.2 = bf16[512,512]{1,0:T(8,128)(2,1)} collective-permute-done((bf16[512,512]{1,0:T(8,128)(2,1)}, bf16[512,512]{1,0:T(8,128)(2,1)}, u32[]{:S(2)}, u32[]{:S(2)}) %collective-permute-start.2) | collective-permute-done | bytes 524320 | tf_op jit(solution)/shard_map/ppermute | solution.py:24
  590.3 15.9 %all-to-all-start.1 = ((f32[128,2,512]{2,1,0:T(2,128)}), f32[128,2,512]{2,1,0:T(2,128)}, u32[]{:S(2)}, u32[]{:S(2)}) async-start(f32[128,2,512]{2,1,0:T(2,128)} %copy.16), calls=%async_computation.1 | async-start | bytes 1048576 | tf_op jit(solution)/shard_map/all_to_all | solution.py:111
  612.4 27.0 %all-to-all-done.1 = f32[128,2,512]{2,1,0:T(2,128)} async-done(((f32[128,2,512]{2,1,0:T(2,128)}), f32[128,2,512]{2,1,0:T(2,128)}, u32[]{:S(2)}, u32[]{:S(2)}) %all-to-all-start.1) | async-done | bytes 524320 | tf_op jit(solution)/shard_map/all_to_all | solution.py:111
  639.4 6.3 all-to-all-start.6
  647.8 53.5 %all-to-all-done.6 = f32[128,1,2048]{2,1,0:T(1,128)S(1)} async-done(((f32[128,1,2048]{2,1,0:T(1,128)}), f32[128,1,2048]{2,1,0:T(1,128)S(1)}, u32[]{:S(2)}, u32[]{:S(2)}) %all-to-all-start.6) | async-done | bytes 1048608 | tf_op jit(solution)/shard_map/all_to_all | solution.py:151
  701.4 6.4 all-to-all-start.8
  714.5 49.0 %all-to-all-done.8 = f32[128,1,2048]{2,1,0:T(1,128)S(1)} async-done(((f32[128,1,2048]{2,1,0:T(1,128)}), f32[128,1,2048]{2,1,0:T(1,128)S(1)}, u32[]{:S(2)}, u32[]{:S(2)}) %all-to-all-start.8) | async-done | bytes 1048608 | tf_op jit(solution)/shard_map/all_to_all | solution.py:152
  (71 shorter events, 75.3 us)
Async XLA Ops:
  14.0 75.1 %all-to-all-start = ((bf16[128,2,2048]{2,1,0:T(2,128)(2,1)}), bf16[128,2,2048]{2,1,0:T(2,128)(2,1)S(1)}, u32[]{:S(2)}, u32[]{:S(2)}) async-start(bf16[128,2,2048]{2,1,0:T(2,128)(2,1)} %reshape.99), calls=%async_computation | async-start | bytes 2097152 | tf_op jit(solution)/shard_map/all_to_all | solution.py:89
  89.1 29.0 %all-to-all-start.2 = ((bf16[128,2,512]{2,1,0:T(2,128)(2,1)}), bf16[128,2,512]{2,1,0:T(2,128)(2,1)S(1)}, u32[]{:S(2)}, u32[]{:S(2)}) async-start(bf16[128,2,512]{2,1,0:T(2,128)(2,1)} %reshape.101), calls=%async_computation.2 | async-start | bytes 524288 | tf_op jit(solution)/shard_map/all_to_all | solution.py:96
  95.6 70.7 %reduce-scatter.2.cloned.1.call-start = ((), (), s32[]{:S(2)}) async-start(), calls=%async_computation.10 | async-start | bytes 5242880 | tf_op jit(solution)/shard_map/reduce_scatter | solution.py:120
  120.8 120.3 %copy-start.5 = (s32[128]{0:T(128)S(1)}, s32[128]{0:T(128)}, u32[]{:S(2)}) copy-start(s32[128]{0:T(128)} %param.14) | copy-start | bytes 1540
  120.8 251.8 %all-reduce.3.cloned.1.call-start = ((), (), s32[]{:S(2)}) async-start(), calls=%async_computation.11 | async-start | bytes 2097152 | tf_op jit(solution)/shard_map/psum | solution.py:54
  321.4 122.1 %all-reduce.5.cloned.1.call-start = ((), (), s32[]{:S(2)}) async-start(), calls=%async_computation.12 | async-start | bytes 2097152 | tf_op jit(solution)/shard_map/psum | solution.py:57
  381.2 66.3 %copy-start = (f32[1,512,512]{2,1,0:T(8,128)S(1)}, f32[1,512,512]{2,1,0:T(8,128)}, u32[]{:S(2)}) copy-start(f32[1,512,512]{2,1,0:T(8,128)} %param.13) | copy-start | bytes 3145732
  450.8 21.7 %copy-start.1 = (f32[512,512]{1,0:T(8,128)S(1)}, f32[512,512]{1,0:T(8,128)}, u32[]{:S(2)}) copy-start(f32[512,512]{1,0:T(8,128)} %get-tuple-element.12) | copy-start | bytes 3145732
  454.3 73.8 %all-to-all-start.7 = ((f32[128,1,2048]{2,1,0:T(1,128)}), f32[128,1,2048]{2,1,0:T(1,128)S(1)}, u32[]{:S(2)}, u32[]{:S(2)}) async-start(f32[128,1,2048]{2,1,0:T(1,128)} %all_to_all.71), calls=%async_computation.8 | async-start | bytes 2097152 | tf_op jit(solution)/shard_map/all_to_all | solution.py:144
  528.1 6.9 copy-start.2
  528.1 62.2 %all-to-all-start.5 = ((f32[128,1,2048]{2,1,0:T(1,128)}), f32[128,1,2048]{2,1,0:T(1,128)}, u32[]{:S(2)}, u32[]{:S(2)}) async-start(f32[128,1,2048]{2,1,0:T(1,128)} %all_to_all.70), calls=%async_computation.6 | async-start | bytes 2097152 | tf_op jit(solution)/shard_map/all_to_all | solution.py:141
  536.5 16.4 %collective-permute-start = (bf16[512,512]{1,0:T(8,128)(2,1)S(1)}, bf16[512,512]{1,0:T(8,128)(2,1)S(1)}, u32[]{:S(2)}, u32[]{:S(2)}) collective-permute-start(bf16[512,512]{1,0:T(8,128)(2,1)S(1)} %get-tuple-element.10), channel_id=1, source_target_pairs={{0,1},{1,2},{2,3},{3,0},{4,5},{5,6},{6,7},{7,4},{8,9},{9,10},{10,1... | collective-permute-start | bytes 1572872 | tf_op jit(solution)/shard_map/ppermute | solution.py:24
  552.8 0.8 copy-start.4
  553.7 15.5 %collective-permute-start.1 = (bf16[512,512]{1,0:T(8,128)(2,1)S(1)}, bf16[512,512]{1,0:T(8,128)(2,1)}, u32[]{:S(2)}, u32[]{:S(2)}) collective-permute-start(bf16[512,512]{1,0:T(8,128)(2,1)S(1)} %collective-permute-done), channel_id=1, source_target_pairs={{0,1},{1,2},{2,3},{3,0},{4,5},{5,6},{6,7},{7,4},{8,9},{9,10},{10,1... | collective-permute-start | bytes 1572872 | tf_op jit(solution)/shard_map/ppermute | solution.py:24
  569.2 14.8 %collective-permute-start.2 = (bf16[512,512]{1,0:T(8,128)(2,1)}, bf16[512,512]{1,0:T(8,128)(2,1)}, u32[]{:S(2)}, u32[]{:S(2)}) collective-permute-start(bf16[512,512]{1,0:T(8,128)(2,1)} %collective-permute-done.1), channel_id=1, source_target_pairs={{0,1},{1,2},{2,3},{3,0},{4,5},{5,6},{6,7},{7,4},{8,9},{9,10},{10,1... | collective-permute-start | bytes 1572872 | tf_op jit(solution)/shard_map/ppermute | solution.py:24
  585.8 20.4 %copy-start.3 = (f32[128,1,2048]{2,1,0:T(1,128)S(1)}, f32[128,1,2048]{2,1,0:T(1,128)}, u32[]{:S(2)}) copy-start(f32[128,1,2048]{2,1,0:T(1,128)} %copy-done.2) | copy-start | bytes 3145732
  590.3 49.1 %all-to-all-start.1 = ((f32[128,2,512]{2,1,0:T(2,128)}), f32[128,2,512]{2,1,0:T(2,128)}, u32[]{:S(2)}, u32[]{:S(2)}) async-start(f32[128,2,512]{2,1,0:T(2,128)} %copy.16), calls=%async_computation.1 | async-start | bytes 1048576 | tf_op jit(solution)/shard_map/all_to_all | solution.py:111
  639.4 62.0 %all-to-all-start.6 = ((f32[128,1,2048]{2,1,0:T(1,128)}), f32[128,1,2048]{2,1,0:T(1,128)S(1)}, u32[]{:S(2)}, u32[]{:S(2)}) async-start(f32[128,1,2048]{2,1,0:T(1,128)} %copy.22), calls=%async_computation.7 | async-start | bytes 2097152 | tf_op jit(solution)/shard_map/all_to_all | solution.py:151
  701.4 62.1 %all-to-all-start.8 = ((f32[128,1,2048]{2,1,0:T(1,128)}), f32[128,1,2048]{2,1,0:T(1,128)S(1)}, u32[]{:S(2)}, u32[]{:S(2)}) async-start(f32[128,1,2048]{2,1,0:T(1,128)} %copy.24), calls=%async_computation.9 | async-start | bytes 2097152 | tf_op jit(solution)/shard_map/all_to_all | solution.py:152
Sparse Core Ops, SparseCore 0:
  120.9 45.3 reduce-scatter.1
  321.5 51.0 all-reduce.2
  381.3 62.1 all-reduce.4
